TPU v7x, 256 devices: a whole 4x4x8 slice. The times are simulated.
256 devices in a mesh: row: 8 (over y, core), col: 16 (over z, x_lo), feat: 2 (over x_hi).
Axes of the slice: x: 4 (x_hi: 2, x_lo: 2; x = x_hi * 2 + x_lo), y: 4, z: 8, core: 2. Of those that a mesh axis runs over, the one named last changes fastest.
Arguments:
- features: bfloat16 [49152, 256], P(('col', 'row')), may hold values from -6 to 6
- weight: bfloat16 [256, 256], P(None, 'feat'), may hold values from -0.375 to 0.375
- bias: float32 [256], P('feat'), may hold values from -3 to 3
- blocks: bfloat16 [8, 16, 192, 128, 128], P('row', 'col'), may hold values from -0.09375 to 0.09375
- coords: int32 [8, 16, 192, 2], P('row', 'col'), may hold values from 0 to 47, as said below
- counts: int32 [8, 16], P('row', 'col'), may hold values from 24 to 192, as said below
- cotangent: bfloat16 [49152, 256], P(('row', 'col'), 'feat'), may hold values from -6 to 6
Outputs:
- outputs: bfloat16 [49152, 256], P(('row', 'col'), 'feat')
- grad_in: bfloat16 [49152, 256], P(('col', 'row', 'feat'))
- grad_w: float32 [256, 256], P(None, 'feat')
- grad_b: float32 [256], P('feat')
Inputs may be any that keep to these rules, and one draw needn't show every extreme that they name: coords[..., 0] is below 48 and coords[..., 1] is below 24. `counts`: each tile has between 24 and 192 live slots; some tile has 192, some 192 // 8.
All inputs are finite; a program needn't handle non-finite values.
Results may differ from a plain program's by a relative error of at most 0.007.
Values may be sent and summed in bfloat16 or wider, within the bound.
A program may use at most 128 MiB of HBM per device.

v0:
```python
import jax
import jax.numpy as jnp
from jax import lax
from jax.sharding import PartitionSpec as P

CB = 24


def spread(block_set, take_index, put_index, active, source, segment_count, transpose):
    block_size = block_set.shape[-1]
    feature_width = source.shape[1]
    pieces = source.reshape(-1, block_size, feature_width)[take_index]
    einsum_form = "kji,kjf->kif" if transpose else "kij,kjf->kif"
    products = jnp.einsum(einsum_form, block_set, pieces, preferred_element_type=jnp.float32)
    targets = jnp.where(active, put_index, segment_count)
    summed = jax.ops.segment_sum(products, targets, num_segments=segment_count + 1)
    return summed[:segment_count].reshape(segment_count * block_size, feature_width)


def body(features, weight, bias, blocks, coords, counts, cotangent):
    row_count = lax.axis_size("row")
    col_count = lax.axis_size("col")
    row_blocks = CB * col_count // row_count
    block_set = blocks[0, 0]
    row_index = coords[0, 0, :, 0]
    col_index = coords[0, 0, :, 1]
    active = jnp.arange(block_set.shape[0], dtype=jnp.int32) < counts[0, 0]
    gathered = lax.all_gather(features, "row", axis=0, tiled=True)
    col_xw = jnp.dot(gathered, weight, preferred_element_type=jnp.float32).astype(jnp.bfloat16)
    partial_value = spread(block_set, col_index, row_index, active, col_xw, row_blocks, False)
    pre_act = lax.psum_scatter(partial_value, "col", scatter_dimension=0, tiled=True) + bias
    sigmoid_z = jax.nn.sigmoid(pre_act)
    outputs = (pre_act * sigmoid_z).astype(jnp.bfloat16)
    grad_z = (
        cotangent.astype(jnp.float32) * sigmoid_z * (1.0 + pre_act * (1.0 - sigmoid_z))
    ).astype(jnp.bfloat16)
    row_grads = lax.all_gather(grad_z, "col", axis=0, tiled=True)
    grad_cols = spread(block_set, row_index, col_index, active, row_grads, CB, True)
    grad_xw = lax.psum_scatter(grad_cols, "row", scatter_dimension=0, tiled=True).astype(
        jnp.bfloat16
    )
    partials = jnp.einsum("no,fo->nf", grad_xw, weight, preferred_element_type=jnp.float32)
    grad_in = lax.psum_scatter(partials, "feat", scatter_dimension=0, tiled=True).astype(
        jnp.bfloat16
    )
    weight_part = jnp.einsum("nf,no->fo", features, grad_xw, preferred_element_type=jnp.float32)
    bias_part = jnp.sum(grad_z.astype(jnp.float32), axis=0)
    grad_w, grad_b = lax.psum((weight_part, bias_part), ("row", "col"))
    return (outputs, grad_in, grad_w, grad_b)


def solution(mesh):
    in_specs = (
        P(("col", "row"), None),
        P(None, "feat"),
        P("feat"),
        P("row", "col", None, None, None),
        P("row", "col", None, None),
        P("row", "col"),
        P(("row", "col"), "feat"),
    )
    out_specs = (
        P(("row", "col"), "feat"),
        P(("col", "row", "feat"), None),
        P(None, "feat"),
        P("feat"),
    )
    return jax.shard_map(body, mesh=mesh, in_specs=in_specs, out_specs=out_specs, check_vma=False)
```

profile of v0, /device:TPU:1, one launch (start us, length us, event | category | flops | bytes accessed | tf_op | source)
XLA Modules:
  0.0 1316.6 jit_solution(1925601138412320407)
XLA Ops:
  8.6 0.8 compare_select_fusion
  9.4 31.6 %all-gather.3.cloned.1.call-done = bf16[3072,256]{1,0:T(8,128)(2,1)} async-done(((bf16[384,256]{1,0:T(8,128)(2,1)}), bf16[3072,256]{1,0:T(8,128)(2,1)}) %all-gather.3.cloned.1.call-update) | async-done | bytes 1572880 | tf_op jit(solution)/shard_map/all_gather | solution.py:28
  41.0 2.0 convolution_convert_fusion
  43.0 8.0 gather_fusion
  51.0 13.7 %fusion.4 = f32[192,128,128]{1,2,0:T(8,128)} fusion(bf16[192,128,128]{2,1,0:T(8,128)(2,1)} %gather_fusion, bf16[1,1,192,128,128]{4,3,2,1,0:T(8,128)(2,1)} %param.10), kind=kOutput, calls=%fused_computation.8 | convolution fusion | flops 805306368 | bytes 25165824 | tf_op jit(solution)/shard_map/kij,kjf->kif/dot_general | solution.py:14
  64.7 12.6 copy.15
  77.6 25.3 %scatter_fusion = f32[49,128,128]{2,1,0:T(8,128)S(1)} fusion(f32[49,128,128]{2,1,0:T(8,128)S(1)} %broadcast_in_dim.16, s32[192]{0:T(256)S(1)} %bitcast.42, f32[192,128,128]{2,1,0:T(8,128)} %copy.15), kind=kCustom, calls=%fused_computation.2 | custom fusion | flops 3145728 | bytes 37749504 | tf_op jit(solution)/shard_map/scatter-add | solution.py:16
  103.0 1.9 slice.20
  104.9 76.8 %reduce-scatter.4.cloned.1.call-done = f32[384,128]{1,0:T(8,128)} async-done(((f32[6144,128]{1,0:T(8,128)}), f32[384,128]{1,0:T(8,128)}) %reduce-scatter.4.cloned.1.call-update) | async-done | bytes 196624 | tf_op jit(solution)/shard_map/reduce_scatter | solution.py:31
  181.7 1.7 convert_reduce_fusion
  183.7 64.6 %all-gather.5.cloned.1.call-done = bf16[6144,128]{1,0:T(8,128)(2,1)} async-done(((bf16[384,128]{1,0:T(8,128)(2,1)}), bf16[6144,128]{1,0:T(8,128)(2,1)}) %all-gather.5.cloned.1.call-update) | async-done | bytes 1572880 | tf_op jit(solution)/shard_map/all_gather | solution.py:37
  248.3 9.4 gather_fusion.1
  257.7 11.4 fusion.7
  269.0 12.6 copy.17
  281.8 25.3 %scatter_fusion.1 = f32[25,128,128]{2,1,0:T(8,128)S(1)} fusion(f32[25,128,128]{2,1,0:T(8,128)S(1)} %broadcast_in_dim.18, s32[192]{0:T(256)S(1)} %bitcast.41, f32[192,128,128]{2,1,0:T(8,128)} %copy.17), kind=kCustom, calls=%fused_computation.3 | custom fusion | flops 3145728 | bytes 37749504 | tf_op jit(solution)/shard_map/scatter-add | solution.py:16
  307.1 1.3 slice.21
  308.4 42.8 %reduce-scatter.6.cloned.1.call-done = f32[384,128]{1,0:T(8,128)} async-done(((f32[3072,128]{1,0:T(8,128)}), f32[384,128]{1,0:T(8,128)}) %reduce-scatter.6.cloned.1.call-update) | async-done | bytes 196624 | tf_op jit(solution)/shard_map/reduce_scatter | solution.py:39
  351.3 1.8 convolution_bitcast_fusion
  353.2 1.9 fusion.11
  355.1 261.2 %psum.15 = f32[128]{0:T(128)} all-reduce(f32[128]{0:T(128)S(1)} %get-tuple-element.12), channel_id=1, replica_groups=mesh['row'=8,'col'=16,'feat'=2] {'row','col'}, use_global_device_ids=true, to_apply=%region_7.8 | all-reduce | flops 128 | bytes 1024 | tf_op jit(solution)/shard_map/psum | solution.py:48
  616.2 660.7 %all-reduce.2.cloned.1.call-done = f32[256,128]{0,1:T(8,128)} async-done(((f32[256,128]{0,1:T(8,128)}), f32[256,128]{0,1:T(8,128)}) %all-reduce.2.cloned.1.call-update) | async-done | bytes 131088 | tf_op jit(solution)/shard_map/psum | solution.py:48
  1276.9 1.7 copy.18
  1278.6 29.6 %reduce-scatter.8.cloned.1.call-done = f32[192,256]{1,0:T(8,128)} async-done(((f32[384,256]{1,0:T(8,128)}), f32[192,256]{1,0:T(8,128)}) %reduce-scatter.8.cloned.1.call-update) | async-done | bytes 196624 | tf_op jit(solution)/shard_map/reduce_scatter | solution.py:43
  1308.2 1.6 convert_element_type.26
  (24 shorter events, 1.8 us)
Async XLA Ops:
  7.2 33.8 %copy-start = (bf16[256,128]{1,0:T(8,128)(2,1)S(1)}, bf16[256,128]{1,0:T(8,128)(2,1)}, u32[]{:S(2)}) copy-start(bf16[256,128]{1,0:T(8,128)(2,1)} %param.8) | copy-start | bytes 196612
  7.2 33.8 %all-gather.3.cloned.1.call-start = ((), (), s32[]{:S(2)}) async-start(), calls=%async_computation.3 | async-start | bytes 1769472 | tf_op jit(solution)/shard_map/all_gather | solution.py:28
  7.9 173.8 %reduce-scatter.4.cloned.1.call-start = ((), (), s32[]{:S(2)}) async-start(), calls=%async_computation.4 | async-start | bytes 3342336 | tf_op jit(solution)/shard_map/reduce_scatter | solution.py:31
  102.9 78.7 %copy-start.2 = (bf16[384,128]{1,0:T(8,128)(2,1)S(1)}, bf16[384,128]{1,0:T(8,128)(2,1)}, u32[]{:S(2)}) copy-start(bf16[384,128]{1,0:T(8,128)(2,1)} %param.13) | copy-start | bytes 294916
  103.0 78.7 %copy-start.3 = (f32[128]{0:T(128)S(1)}, f32[128]{0:T(128)}, u32[]{:S(2)}) copy-start(f32[128]{0:T(128)} %param.9) | copy-start | bytes 1540
  104.9 143.4 %all-gather.5.cloned.1.call-start = ((), (), s32[]{:S(2)}) async-start(), calls=%async_computation.5 | async-start | bytes 1671168 | tf_op jit(solution)/shard_map/all_gather | solution.py:37
  183.4 167.9 %reduce-scatter.6.cloned.1.call-start = ((), (), s32[]{:S(2)}) async-start(), calls=%async_computation.6 | async-start | bytes 1769472 | tf_op jit(solution)/shard_map/reduce_scatter | solution.py:39
  281.8 69.5 %copy-start.1 = (bf16[384,256]{1,0:T(8,128)(2,1)S(1)}, bf16[384,256]{1,0:T(8,128)(2,1)}, u32[]{:S(2)}) copy-start(bf16[384,256]{1,0:T(8,128)(2,1)} %param.7) | copy-start | bytes 589828
  308.4 968.6 %all-reduce.2.cloned.1.call-start = ((), (), s32[]{:S(2)}) async-start(), calls=%async_computation.8 | async-start | bytes 262144 | tf_op jit(solution)/shard_map/psum | solution.py:48
  353.1 955.1 %reduce-scatter.8.cloned.1.call-start = ((), (), s32[]{:S(2)}) async-start(), calls=%async_computation.7 | async-start | bytes 589824 | tf_op jit(solution)/shard_map/reduce_scatter | solution.py:43
Sparse Core Ops, SparseCore 0:
  9.8 31.1 all-gather.2
  105.0 76.6 reduce-scatter.3
  184.0 64.1 all-gather.4
  308.5 42.7 reduce-scatter.5
  354.3 922.5 all-reduce.1
  1279.5 28.6 reduce-scatter.7
where the time goes:
time: 1320 us
  waiting for transfers between devices  907 us (69%)
  blocking collectives  261 us (20%)
  other arithmetic  54.6 us (4%)
  local copies, waits for them, and re-layouts  47.9 us (4%)
  matrix products  30.7 us (2%)
  between operations  14.8 us (1%)
    psum x1, waiting for transfers between devices, body(): grad_w, grad_b = lax.psum((weight_part, bias_part), ('row', 'col'))  661 us
    psum x1, blocking collectives, body(): grad_w, grad_b = lax.psum((weight_part, bias_part), ('row', 'col'))  261 us
    reduce_scatter x1, waiting for transfers between devices, body(): lax.psum_scatter(partial_value, 'col', scatter_dimension=0, tiled=True)  76.8 us
    all_gather x1, waiting for transfers between devices, body(): row_grads = lax.all_gather(grad_z, 'col', axis=0, tiled=True)  64.6 us
    scatter-add x2, other arithmetic, spread(): jax.ops.segment_sum(products, targets, num_segments=segment_count + 1)  50.6 us
    reduce_scatter x1, waiting for transfers between devices, body(): lax.psum_scatter(grad_cols, 'row', scatter_dimension=0, tiled=True)  42.8 us
    all_gather x1, waiting for transfers between devices, body(): gathered = lax.all_gather(features, 'row', axis=0, tiled=True)  31.6 us
    reduce_scatter x1, waiting for transfers between devices, body(): lax.psum_scatter(partials, 'feat', scatter_dimension=0, tiled=True)  29.6 us
  transfers between devices with their start and end apart: 6, of which 6 were waited for; matrix products, arithmetic and copies ran while one was open for 0% of the time, Pallas kernels for 0%

commit v1 on v0

v1 whole, which is shorter than its diff:
```python
import functools

import jax
import jax.numpy as jnp
from jax import lax
from jax.experimental import pallas as pl
from jax.experimental.pallas import tpu as pltpu
from jax.sharding import PartitionSpec as P

BF = jnp.bfloat16
F32 = jnp.float32
MESH = pl.DeviceIdType.MESH
VMEM = pl.BlockSpec(memory_space=pltpu.VMEM)
SMEM = pl.BlockSpec(memory_space=pltpu.SMEM)
ANY = pl.BlockSpec(memory_space=pl.ANY)
LIMIT = 56 * 1024 * 1024
UNROLL = 8


class Net:
    def __init__(self, send_sems, recv_sems):
        self.send_sems, self.recv_sems, self.copies = send_sems, recv_sems, []

    def send(self, src, dst, device):
        index = len(self.copies)
        copy = pltpu.make_async_remote_copy(
            src_ref=src,
            dst_ref=dst,
            send_sem=self.send_sems.at[index],
            recv_sem=self.recv_sems.at[index],
            device_id=device,
            device_id_type=MESH,
        )
        copy.start()
        self.copies.append(copy)
        return copy

    def drain(self):
        for copy in self.copies:
            copy.wait_send()


def greet(devices):
    barrier = pltpu.get_barrier_semaphore()
    for device in devices:
        pl.semaphore_signal(barrier, inc=1, device_id=device, device_id_type=MESH)
    return lambda: pl.semaphore_wait(barrier, len(devices))


def interleave(streams):
    streams = list(streams)
    while streams:
        alive = []
        for stream in streams:
            try:
                next(stream)
                alive.append(stream)
            except StopIteration:
                pass
        streams = alive


def wrap(index, size):
    return lax.rem(index + 2 * size, size)


def gather_xw(feat_ref, w_ref, xw_ref, wfull_ref, send_sems, recv_sems):
    row = lax.axis_index("row")
    y, core = row // 2, lax.rem(row, 2)
    f = lax.axis_index("feat")
    sib = {"row": y * 2 + 1 - core}
    up = {"row": wrap(y + 1, 4) * 2 + core}
    down = {"row": wrap(y - 1, 4) * 2 + core}
    other = {"feat": 1 - f}
    wait = greet([sib, up, down, other])
    xw_ref[row] = jnp.dot(feat_ref[...], w_ref[...], preferred_element_type=F32).astype(BF)
    wfull_ref[f] = w_ref[...]
    wait()
    net = Net(send_sems, recv_sems)
    half = [pl.ds(0, 192), pl.ds(192, 192)]

    def move(slot, part, device):
        ref = xw_ref.at[slot, half[part]]
        return net.send(ref, ref, device)

    u = [move(row, 0, up), None]
    d = [None, move(row, 1, down)]
    u[1] = move(row, 1, up)
    d[0] = move(row, 0, down)
    s = [move(row, 0, sib), move(row, 1, sib)]
    wcopy = net.send(w_ref, wfull_ref.at[f], other)
    lower = wrap(y - 1, 4) * 2 + core
    upper = wrap(y + 1, 4) * 2 + core
    far = wrap(y + 2, 4) * 2 + core
    u[0].wait_recv()
    u2 = move(lower, 0, up)
    s.append(move(lower, 0, sib))
    d[1].wait_recv()
    d2 = move(upper, 1, down)
    s.append(move(upper, 1, sib))
    u[1].wait_recv()
    s.append(move(lower, 1, sib))
    d[0].wait_recv()
    s.append(move(upper, 0, sib))
    u2.wait_recv()
    s.append(move(far, 0, sib))
    d2.wait_recv()
    s.append(move(far, 1, sib))
    wcopy.wait_recv()
    for copy in s:
        copy.wait_recv()
    net.drain()


def spmm(count_ref, coord_ref, src_ref, blocks_ref, out_ref, blk, acc, sems, *, transpose):
    slots = blk.shape[0]
    parts = sems.shape[0]
    size = slots // parts
    targets = out_ref.shape[0]

    def fetch(part):
        span = pl.ds(part * size, size)
        return pltpu.make_async_copy(blocks_ref.at[span], blk.at[span], sems.at[part])

    for part in range(parts):
        fetch(part).start()
    acc[...] = jnp.zeros_like(acc)
    count = count_ref[0]

    def chunk(part, carry):
        fetch(part).wait()
        base = part * size
        groups = jnp.clip((count - base + UNROLL - 1) // UNROLL, 0, size // UNROLL)

        def group(g, carry):
            start = base + g * UNROLL
            for u in range(UNROLL):
                k = start + u
                i, j = coord_ref[0, k], coord_ref[1, k]
                take, put = (i, j) if transpose else (j, i)
                put = jnp.where(k < count, put, targets)
                if transpose:
                    prod = jnp.dot(src_ref[take], blk[k], preferred_element_type=F32)
                else:
                    prod = jnp.dot(blk[k], src_ref[take], preferred_element_type=F32)
                acc[put] += prod
            return carry

        return lax.fori_loop(0, groups, group, carry)

    lax.fori_loop(0, parts, chunk, 0)

    def cast(t, carry):
        out_ref[t] = acc[t].astype(BF)
        return carry

    lax.fori_loop(0, targets, cast, 0)


def call_spmm(count, coord, src, blocks, targets, transpose):
    parts = 8
    return pl.pallas_call(
        functools.partial(spmm, transpose=transpose),
        out_shape=jax.ShapeDtypeStruct((targets, 128, 128), BF),
        in_specs=[SMEM, SMEM, VMEM, ANY],
        out_specs=VMEM,
        scratch_shapes=[
            pltpu.VMEM(blocks.shape, BF),
            pltpu.VMEM((targets + 1, 128, 128), F32),
            pltpu.SemaphoreType.DMA((parts,)),
        ],
        compiler_params=pltpu.CompilerParams(vmem_limit_bytes=LIMIT),
        name="spmm_bwd" if transpose else "spmm_fwd",
    )(count, coord, src, blocks)


def middle(p_ref, bias_ref, cot_ref, out_ref, g_ref, bsum_ref, rp, rm, sp, sm, xr, xs, send_sems, recv_sems):
    col = lax.axis_index("col")
    z, x = col // 2, lax.rem(col, 2)
    nbr = {"col": z * 2 + 1 - x}
    up = {"col": wrap(z + 1, 8) * 2 + x}
    down = {"col": wrap(z - 1, 8) * 2 + x}
    greet([nbr, up, down])()
    net = Net(send_sems, recv_sems)
    A, B, ALL = pl.ds(0, 64), pl.ds(64, 64), pl.ds(0, 128)

    def part(c, b, rows=ALL):
        return p_ref[c, b, rows].astype(F32)

    def ring_z(b, width, own):
        last = None
        for t in range(4):
            du, dd = wrap(z + 4 - t, 8), wrap(z - 4 + t, 8)
            if t:
                yield
                last[0].wait_recv()
                last[1].wait_recv()
            for i in range(width):
                if t == 0:
                    sp[b, t, i, A] = own(du, i, A, t, 0).astype(BF)
                    sm[b, t, i, B] = own(dd, i, B, t, 1).astype(BF)
                elif t == 1:
                    sp[b, t, i, A] = (own(du, i, A, t, 0) + rp[b, 0, i, A].astype(F32)).astype(BF)
                    sp[b, t, i, B] = own(du, i, B, t, 0).astype(BF)
                    sm[b, t, i, A] = own(dd, i, A, t, 1).astype(BF)
                    sm[b, t, i, B] = (own(dd, i, B, t, 1) + rm[b, 0, i, B].astype(F32)).astype(BF)
                else:
                    sp[b, t, i] = (own(du, i, ALL, t, 0) + rp[b, t - 1, i].astype(F32)).astype(BF)
                    sm[b, t, i] = (own(dd, i, ALL, t, 1) + rm[b, t - 1, i].astype(F32)).astype(BF)
            span = pl.ds(0, width)
            rows = (A, B) if t == 0 else (ALL, ALL)
            last = (
                net.send(sp.at[b, t, span, rows[0]], rp.at[b, t, span, rows[0]], up),
                net.send(sm.at[b, t, span, rows[1]], rm.at[b, t, span, rows[1]], down),
            )
        yield
        last[0].wait_recv()
        last[1].wait_recv()

    def reduce_z_first(b):
        yield from ring_z(b, 2, lambda d, i, rows, t, side: part(d * 2 + i, b, rows))

        def full(i):
            return part(z * 2 + i, b) + rp[b, 3, i].astype(F32) + rm[b, 3, i].astype(F32)

        xs[b] = full(1 - x).astype(BF)
        copy = net.send(xs.at[b], xr.at[b, 0], nbr)
        mine = full(x)
        yield
        copy.wait_recv()
        return mine + xr[b, 0].astype(F32)

    def reduce_x_first(b):
        copies = {}
        for k in (4, 3, -3, 2, -2, 1, -1, 0):
            d = wrap(z + k, 8)
            copies[k] = net.send(p_ref.at[d * 2 + 1 - x, b], xr.at[b, k % 8], nbr)
        waited = set()

        def own(d, i, rows, t, side):
            k = 0 if t is None else 4 - t if side == 0 or t == 0 else t - 4
            if k not in waited:
                copies[k].wait_recv()
                waited.add(k)
            return part(d * 2 + x, b, rows) + xr[b, k % 8, rows].astype(F32)

        yield
        yield from ring_z(b, 1, own)
        return own(z, 0, ALL, None, 0) + rp[b, 3, 0].astype(F32) + rm[b, 3, 0].astype(F32)

    def activate(b, total):
        rows = pl.ds(b * 128, 128)
        pre = total + bias_ref[...]
        s = 1.0 / (1.0 + jnp.exp(-pre))
        out_ref[rows] = (pre * s).astype(BF)
        gz = (cot_ref[rows].astype(F32) * s * (1.0 + pre * (1.0 - s))).astype(BF).astype(F32)
        bsum_ref[b] = jnp.sum(gz.reshape(16, 8, 128), axis=0)
        g_ref[col, b] = gz.T.astype(BF)

    def gather_z_first(b):
        def move(slot, device, rows=ALL):
            ref = g_ref.at[slot, b, rows]
            return net.send(ref, ref, device)

        to_x = []
        ups, downs = move(col, up), move(col, down)
        to_x.append(move(col, nbr))
        for t in range(1, 5):
            yield
            src = wrap(z - t, 8) * 2 + x
            ups.wait_recv()
            if t < 4:
                ups = move(src, up, ALL if t < 3 else A)
            to_x.append(move(src, nbr, ALL if t < 4 else A))
            src = wrap(z + t, 8) * 2 + x
            downs.wait_recv()
            if t < 4:
                downs = move(src, down, ALL if t < 3 else B)
            to_x.append(move(src, nbr, ALL if t < 4 else B))
        yield
        for copy in to_x:
            copy.wait_recv()

    def gather_x_first(b):
        def move(zz, device, rows=ALL):
            ref = g_ref.at[pl.ds(zz * 2, 2), b, rows]
            return net.send(ref, ref, device)

        ref = g_ref.at[col, b]
        first = net.send(ref, ref, nbr)
        yield
        first.wait_recv()
        ups, downs = move(z, up), move(z, down)
        for t in range(1, 5):
            yield
            ups.wait_recv()
            if t < 4:
                ups = move(wrap(z - t, 8), up, ALL if t < 3 else A)
            downs.wait_recv()
            if t < 4:
                downs = move(wrap(z + t, 8), down, ALL if t < 3 else B)

    def stream(b, reduce, gather):
        total = yield from reduce(b)
        activate(b, total)
        yield from gather(b)

    interleave([
        stream(0, reduce_z_first, gather_x_first),
        stream(1, reduce_x_first, gather_z_first),
        stream(2, reduce_x_first, gather_x_first),
    ])
    net.drain()


def finish(
    p_ref, feat_ref, wfull_ref, bsum_ref, gin_ref, gw_ref, gb_ref,
    cr, rp, rm, sp, sm, g, h, gin, part, w1, w2, w3, wx, xin, send_sems, recv_sems,
):
    row = lax.axis_index("row")
    y, core = row // 2, lax.rem(row, 2)
    col = lax.axis_index("col")
    z, x = col // 2, lax.rem(col, 2)
    f = lax.axis_index("feat")
    sib = {"row": y * 2 + 1 - core}
    up = {"row": wrap(y + 1, 4) * 2 + core}
    down = {"row": wrap(y - 1, 4) * 2 + core}
    other = {"feat": 1 - f}
    rows_of = [{"row": wrap(row + k, 8)} for k in range(1, 8)]
    nbr = {"col": z * 2 + 1 - x}
    zs_of = [{"col": wrap(z + k, 8) * 2 + x} for k in range(1, 8)]
    greet(rows_of + zs_of + [nbr, other])()
    net = Net(send_sems, recv_sems)
    A, B, ALL = pl.ds(0, 64), pl.ds(64, 64), pl.ds(0, 128)

    def reduce(b):
        copies = {}
        for k in (2, 1, -1, 0):
            d = wrap(y + k, 4)
            copies[k] = net.send(p_ref.at[d * 2 + 1 - core, b], cr.at[b, k % 4], sib)
        yield

        def own(k, rows):
            slot = wrap(y + k, 4) * 2 + core
            return p_ref[slot, b, rows].astype(F32) + cr[b, k % 4, rows].astype(F32)

        copies[2].wait_recv()
        sp[b, 0, A] = own(2, A).astype(BF)
        sm[b, 0, B] = own(2, B).astype(BF)
        u = net.send(sp.at[b, 0, A], rp.at[b, 0, A], up)
        d = net.send(sm.at[b, 0, B], rm.at[b, 0, B], down)
        yield
        copies[1].wait_recv()
        u.wait_recv()
        sp[b, 1, A] = (own(1, A) + rp[b, 0, A].astype(F32)).astype(BF)
        sp[b, 1, B] = own(1, B).astype(BF)
        u = net.send(sp.at[b, 1], rp.at[b, 1], up)
        copies[-1].wait_recv()
        d.wait_recv()
        sm[b, 1, A] = own(-1, A).astype(BF)
        sm[b, 1, B] = (own(-1, B) + rm[b, 0, B].astype(F32)).astype(BF)
        d = net.send(sm.at[b, 1], rm.at[b, 1], down)
        yield
        copies[0].wait_recv()
        u.wait_recv()
        d.wait_recv()
        g[b] = (own(0, ALL) + rp[b, 1].astype(F32) + rm[b, 1].astype(F32)).astype(BF)

    interleave([reduce(b) for b in range(3)])

    halves = net.send(g.at[pl.ds(1 - f, 2)], h, other)
    gwt = jnp.zeros((128, 256), F32)
    for b in range(3):
        gwt += jnp.dot(g[b], feat_ref[pl.ds(b * 128, 128)], preferred_element_type=F32)
    for r in range(8):
        part[r, 0:16] = gwt[r * 16:(r + 1) * 16]
        part[r, 16:24, 0:128] = bsum_ref[0] + bsum_ref[1] + bsum_ref[2]
        part[r, 16:24, 128:256] = jnp.zeros((8, 128), F32)
    copies = []
    for k in range(1, 8):
        copies.append(net.send(part.at[wrap(row + k, 8)], w1.at[row], rows_of[k - 1]))
    w1[row] = part[row]

    halves.wait_recv()
    for n in range(2):
        block = jnp.dot(wfull_ref[f], g[f + n], preferred_element_type=F32)
        block += jnp.dot(wfull_ref[1 - f], h[n], preferred_element_type=F32)
        gin[pl.ds(n * 128, 128)] = block.T.astype(BF)
    gin_ref[...] = gin[pl.ds(pl.multiple_of(f * 64, 64), 192)]

    for copy in copies:
        copy.wait_recv()
    total = w1[0]
    for r in range(1, 8):
        total += w1[r]
    wx[...] = total
    copy = net.send(wx, xin, nbr)
    copy.wait_recv()
    w2[z] = wx[...] + xin[...]
    copies = [net.send(w2.at[z], w2.at[z], zs_of[k - 1]) for k in range(1, 8)]
    for copy in copies:
        copy.wait_recv()
    total = w2[0]
    for r in range(1, 8):
        total += w2[r]
    w3[row] = total[0:16]
    gb_ref[...] = jnp.sum(total[16:24, 0:128], axis=0, keepdims=True)
    copies = [net.send(w3.at[row], w3.at[row], rows_of[k - 1]) for k in range(1, 8)]
    for copy in copies:
        copy.wait_recv()
    gw_ref[...] = w3[...].reshape(128, 256).T
    net.drain()


def remote_call(kernel, name, collective_id, out_shape, operands, scratch, copies):
    return pl.pallas_call(
        kernel,
        out_shape=out_shape,
        in_specs=[VMEM] * len(operands),
        out_specs=[VMEM] * len(out_shape),
        scratch_shapes=scratch
        + [pltpu.SemaphoreType.DMA((copies,)), pltpu.SemaphoreType.DMA((copies,))],
        compiler_params=pltpu.CompilerParams(
            collective_id=collective_id, has_side_effects=True, vmem_limit_bytes=LIMIT
        ),
        name=name,
    )(*operands)


def body(features, weight, bias, blocks, coords, counts, cotangent):
    blocks = blocks[0, 0]
    coord = coords[0, 0].T
    count = counts[0]
    shape = jax.ShapeDtypeStruct
    xw, wfull = remote_call(
        gather_xw, "gather_xw", 1,
        [shape((8, 384, 128), BF), shape((2, 256, 128), BF)],
        [features, weight], [], 16,
    )
    partial = call_spmm(count, coord, xw.reshape(24, 128, 128), blocks, 48, False)
    tile = (128, 128)
    outputs, g, bsum = remote_call(
        middle, "middle", 2,
        [shape((384, 128), BF), shape((16, 3) + tile, BF), shape((3, 8, 128), F32)],
        [partial.reshape((16, 3) + tile), bias.reshape(1, 128), cotangent],
        [
            pltpu.VMEM((3, 4, 2) + tile, BF),
            pltpu.VMEM((3, 4, 2) + tile, BF),
            pltpu.VMEM((3, 4, 2) + tile, BF),
            pltpu.VMEM((3, 4, 2) + tile, BF),
            pltpu.VMEM((3, 8) + tile, BF),
            pltpu.VMEM((3,) + tile, BF),
        ],
        80,
    )
    grads = call_spmm(count, coord, g.reshape((48,) + tile), blocks, 24, True)
    grad_in, grad_w, grad_b = remote_call(
        finish, "finish", 3,
        [shape((192, 256), BF), shape((256, 128), F32), shape((1, 128), F32)],
        [grads.reshape((8, 3) + tile), features, wfull, bsum],
        [
            pltpu.VMEM((3, 4) + tile, BF),
            pltpu.VMEM((3, 2) + tile, BF),
            pltpu.VMEM((3, 2) + tile, BF),
            pltpu.VMEM((3, 2) + tile, BF),
            pltpu.VMEM((3, 2) + tile, BF),
            pltpu.VMEM((3,) + tile, BF),
            pltpu.VMEM((2,) + tile, BF),
            pltpu.VMEM((256, 256), BF),
            pltpu.VMEM((8, 24, 256), F32),
            pltpu.VMEM((8, 24, 256), F32),
            pltpu.VMEM((8, 24, 256), F32),
            pltpu.VMEM((8, 16, 256), F32),
            pltpu.VMEM((24, 256), F32),
            pltpu.VMEM((24, 256), F32),
        ],
        50,
    )
    return outputs, grad_in, grad_w, grad_b.reshape(128)


def solution(mesh):
    in_specs = (
        P(("col", "row"), None),
        P(None, "feat"),
        P("feat"),
        P("row", "col", None, None, None),
        P("row", "col", None, None),
        P("row", "col"),
        P(("row", "col"), "feat"),
    )
    out_specs = (
        P(("row", "col"), "feat"),
        P(("col", "row", "feat"), None),
        P(None, "feat"),
        P("feat"),
    )
    return jax.shard_map(body, mesh=mesh, in_specs=in_specs, out_specs=out_specs, check_vma=False)
```

time: 1320 us -> 124 us (0.09)
  waiting for transfers between devices: 907 us -> 0 us
  blocking collectives: 261 us -> 0 us
  Pallas kernels: 0 us -> 117 us
  other arithmetic: 54.6 us -> 0 us
  local copies, waits for them, and re-layouts: 47.9 us -> 4.89 us
  matrix products: 30.7 us -> 0 us
  between operations: 14.8 us -> 1.33 us
    psum x1 -> x0, waiting for transfers between devices: 661 us -> none  [body(): grad_w, grad_b = lax.psum((weight_part, bias_part), ('row', 'col'))]
    psum x1 -> x0, blocking collectives: 261 us -> none  [body(): grad_w, grad_b = lax.psum((weight_part, bias_part), ('row', 'col'))]
    reduce_scatter x3 -> x0, waiting for transfers between devices: 149 us -> none  [the longest x1 76.8 us: body(): lax.psum_scatter(partial_value, 'col', scatter_dimension=0, tiled=True)]
    pallas_call x0 -> x5, Pallas kernels: none -> 117 us  [the longest x3 98.2 us: remote_call(): pl.pallas_call(kernel, out_shape=out_shape, in_specs=[VMEM] * len(operand...]
    all_gather x2 -> x0, waiting for transfers between devices: 96.2 us -> none  [the longest x1 64.6 us: body(): row_grads = lax.all_gather(grad_z, 'col', axis=0, tiled=True)]
    scatter-add x2 -> x0, other arithmetic: 50.6 us -> none  [spread(): jax.ops.segment_sum(products, targets, num_segments=segment_count + 1)]
    dot_general x5 -> x0, matrix products: 30.7 us -> none  [the longest x2 25.1 us: spread(): jnp.einsum(einsum_form, block_set, pieces, preferred_element_type=jnp.flo...]
    dot_general x2 -> x0, local copies, waits for them, and re-layouts: 25.2 us -> none  [spread(): jnp.einsum(einsum_form, block_set, pieces, preferred_element_type=jnp.flo...]
  transfers between devices with their start and end apart: 6 -> 0, of which waited for: 6 -> 0; matrix products, arithmetic and copies ran while one was open for 0% -> 0% of each run, Pallas kernels for 0% -> 0%
where the time goes in v1:
time: 124 us; the launch traced here: 123 us
  Pallas kernels  117 us (94%)
  local copies, waits for them, and re-layouts  4.89 us (4%)
  between operations  1.33 us (1%)
    pallas_call x3, Pallas kernels, remote_call(): pl.pallas_call(kernel, out_shape=out_shape, in_specs=[VMEM] * len(operand...  98.2 us
    pallas_call x2, Pallas kernels, call_spmm(): pl.pallas_call(functools.partial(spmm, transpose=transpose), out_shape=ja...  19 us
    unnamed x6, local copies, waits for them, and re-layouts  4.89 us

profile of v1, /device:TPU:1, one launch (start us, length us, event | category | flops | bytes accessed | tf_op | source)
XLA Modules:
  0.0 123.4 jit_solution(15339055999235011819)
XLA Ops:
  1.3 15.6 %gather_xw.1 = (bf16[8,384,128]{2,1,0:T(8,128)(2,1)}, bf16[2,256,128]{2,1,0:T(8,128)(2,1)}) custom-call(bf16[384,256]{1,0:T(8,128)(2,1)} %feat_ref.3, bf16[256,128]{1,0:T(8,128)(2,1)} %w_ref.1), custom_call_target="tpu_custom_call" | custom-call | tf_op jit(solution)/shard_map/gather_xw/pallas_call | solution.py:416
  16.9 9.6 %spmm_fwd.1 = bf16[48,128,128]{2,1,0:T(8,128)(2,1)} custom-call(s32[1]{0:T(128)} %bitcast.11.count_ref, s32[2,192]{1,0:T(2,128)} %bitcast.19, bf16[24,128,128]{2,1,0:T(8,128)(2,1)} %bitcast.18, bf16[192,128,128]{2,1,0:T(8,128)(2,1)} %bitcast.13), custom_call_target="tpu_custom_call" | custom-call | tf_op jit(solution)/shard_map/spmm_fwd/pallas_call | solution.py:162
  26.5 43.6 %middle.1 = (bf16[384,128]{1,0:T(8,128)(2,1)}, bf16[16,3,128,128]{3,2,1,0:T(8,128)(2,1)}, f32[3,8,128]{2,1,0:T(8,128)}) custom-call(bf16[16,3,128,128]{3,2,1,0:T(8,128)(2,1)} %bitcast.15, f32[1,128]{1,0:T(1,128)} %bitcast.21, bf16[384,128]{1,0:T(8,128)(2,1)} %cot_ref.1), custom_call_target="tpu_custom_call" | custom-call | tf_op jit(solution)/shard_map/middle/pallas_call | solution.py:416
  70.1 0.0 copy-start
  70.1 9.4 %spmm_bwd.1 = bf16[24,128,128]{2,1,0:T(8,128)(2,1)} custom-call(s32[1]{0:T(128)} %bitcast.12.count_ref, s32[2,192]{1,0:T(2,128)} %bitcast.20, bf16[48,128,128]{2,1,0:T(8,128)(2,1)} %bitcast.17, bf16[192,128,128]{2,1,0:T(8,128)(2,1)} %bitcast.14), custom_call_target="tpu_custom_call" | custom-call | tf_op jit(solution)/shard_map/spmm_bwd/pallas_call | solution.py:162
  79.5 39.0 %finish.1 = (bf16[192,256]{1,0:T(8,128)(2,1)}, f32[256,128]{1,0:T(8,128)}, f32[1,128]{1,0:T(1,128)}) custom-call(bf16[8,3,128,128]{3,2,1,0:T(8,128)(2,1)} %bitcast.16, bf16[384,256]{1,0:T(8,128)(2,1)} %feat_ref.3, bf16[2,256,128]{2,1,0:T(8,128)(2,1)} %get-tuple-element.15.wfull_ref, f32[3,8,128]{2,1,0:T(8,128)} %get-tuple-element.16.bsum_ref), custom_call_target="tpu_custom_call" | custom-call | tf_op jit(solution)/shard_map/finish/pallas_call | solution.py:416
  118.5 0.0 copy-done
  118.5 0.6 copy.16
  119.2 1.5 %copy.17 = bf16[192,256]{1,0:T(8,128)(2,1)} copy(bf16[192,256]{1,0:T(8,128)(2,1)} %get-tuple-element.25) | data formatting | bytes 196608
  120.7 1.6 %copy.18 = f32[256,128]{1,0:T(8,128)} copy(f32[256,128]{1,0:T(8,128)} %get-tuple-element.26) | data formatting | bytes 262144
  122.3 1.1 copy.19
Async XLA Ops:
  70.1 48.4 %copy-start = (bf16[384,128]{1,0:T(8,128)(2,1)S(1)}, bf16[384,128]{1,0:T(8,128)(2,1)}, u32[]{:S(2)}) copy-start(bf16[384,128]{1,0:T(8,128)(2,1)} %get-tuple-element.24) | copy-start | bytes 294916

commit v2 on v0

v2 whole, which is shorter than its diff:
```python
import functools

import jax
import jax.numpy as jnp
from jax import lax
from jax.experimental import pallas as pl
from jax.experimental.pallas import tpu as pltpu
from jax.sharding import PartitionSpec as P

BF = jnp.bfloat16
F32 = jnp.float32
MESH = pl.DeviceIdType.MESH
VMEM = pl.BlockSpec(memory_space=pltpu.VMEM)
SMEM = pl.BlockSpec(memory_space=pltpu.SMEM)
ANY = pl.BlockSpec(memory_space=pl.ANY)
LIMIT = 62 * 1024 * 1024


class Net:
    def __init__(self, send_sems, recv_sems):
        self.send_sems, self.recv_sems, self.copies = send_sems, recv_sems, []

    def send(self, src, dst, device):
        index = len(self.copies)
        copy = pltpu.make_async_remote_copy(
            src_ref=src,
            dst_ref=dst,
            send_sem=self.send_sems.at[index],
            recv_sem=self.recv_sems.at[index],
            device_id=device,
            device_id_type=MESH,
        )
        copy.start()
        self.copies.append(copy)
        return copy

    def drain(self):
        for copy in self.copies:
            copy.wait_send()


def greet(devices):
    barrier = pltpu.get_barrier_semaphore()
    for device in devices:
        pl.semaphore_signal(barrier, inc=1, device_id=device, device_id_type=MESH)
    return lambda: pl.semaphore_wait(barrier, len(devices))


def interleave(streams):
    streams = list(streams)
    while streams:
        alive = []
        for stream in streams:
            try:
                next(stream)
                alive.append(stream)
            except StopIteration:
                pass
        streams = alive


def wrap(index, size):
    return lax.rem(index + 2 * size, size)


def order_slots(coord, count, key, targets, lists, work):
    size, half = 256, 128
    work[0:2, :] = jnp.full((2, size), 63.0, F32)
    work[0:2, 0:192] = coord[...].astype(F32)
    one, zero = jnp.float32(1.0), jnp.float32(0.0)
    lane = lax.broadcasted_iota(jnp.int32, (size, size), 1)
    sub = lax.broadcasted_iota(jnp.int32, (size, size), 0)
    keys = jnp.where(lane[0:1] < count, work[key:key + 1, :], 63.0)
    takes = work[1 - key:2 - key, :]
    key_of = jnp.broadcast_to(keys, (half, size)).T
    wide = jnp.concatenate([key_of, key_of], axis=1)
    same = jnp.where(wide == keys, one, zero)
    rank_row = jnp.sum(jnp.where(sub < lane, same, zero), axis=0, keepdims=True)
    rank = jnp.dot(
        jnp.where(lane < sub, same, zero).astype(BF), jnp.ones((size, half), BF), preferred_element_type=F32
    )
    member = jnp.where(key_of == lane[:, :half].astype(F32), one, zero)
    number = jnp.sum(member, axis=0, keepdims=True)
    number = jnp.where(lane[0:1, :half] < targets, number, zero)
    steps = jnp.floor((number + 1.0) * 0.5)
    lower = jnp.where(sub[:half, :half] < lane[:half, :half], one, zero).astype(BF)
    start = jnp.dot(jnp.broadcast_to(steps, (half, half)).astype(BF), lower, preferred_element_type=F32)
    start_of = lax.dot_general(
        member.astype(BF), start.astype(BF), (((1,), (1,)), ((), ())), preferred_element_type=F32
    )
    place = jnp.where(key_of > 62.0, -1.0, 2.0 * start_of + rank)
    lane_f = lane.astype(F32)
    hit = jnp.where(jnp.concatenate([place, place], axis=1) == lane_f, one, zero).astype(BF)
    kind = sub[0:16]
    opens = jnp.where(rank_row == 0.0, one, zero)
    values = jnp.where(kind == 0, lane_f[0:16] - 192.0, jnp.where(kind == 1, takes, jnp.where(kind == 2, opens, zero)))
    found = jnp.dot(values.astype(BF), hit, preferred_element_type=F32).astype(jnp.int32)
    lists[0:1, :] = jnp.clip(found[0:1] + 192, 0, 192)
    lists[1:2, :] = jnp.clip(found[1:2], 0, 71 - targets)
    lists[2:3, :] = jnp.clip(found[2:3], 0, 1)
    lists[3:4, 0:half] = jnp.clip((start[0:1] + steps - 1.0).astype(jnp.int32), 0, 95 + targets // 2)
    lists[4:5, 0:half] = jnp.where(number > 0.0, 1, 0)


def products(table, blk, src, run_of, steps, unroll, transpose):
    def group(i, run):
        for u in range(unroll):
            q = i * unroll + u
            s0, s1 = table[0, 2 * q], table[0, 2 * q + 1]
            t0, t1 = table[1, 2 * q], table[1, 2 * q + 1]
            if transpose:
                lhs = jnp.concatenate([src[t0], src[t1]], axis=1)
                rhs = jnp.concatenate([blk[s0], blk[s1]], axis=0)
            else:
                lhs = jnp.concatenate([blk[s0], blk[s1]], axis=1)
                rhs = jnp.concatenate([src[t0], src[t1]], axis=0)
            prod = jnp.dot(lhs, rhs, preferred_element_type=F32)
            run = jnp.where(table[2, 2 * q] == 1, 0.0, run) + prod
            run_of[q] = run
        return run

    lax.fori_loop(0, steps // unroll, group, jnp.zeros((128, 128), F32))


def layer(
    feat_ref, w_ref, bias_ref, coord_ref, count_ref, cot_ref, blocks_ref,
    out_ref, gin_ref, gw_ref, gb_ref,
    xw, fall, wfull, blk, run_of, p, g, rp, rm, sp, sm, dp, dm, xr,
    p5, cr, rp5, sp5, g5, h, gin, part5, w1, w2, w3, bsend, brecv,
    coord, bias, cot, work, lists, table, send_sems, recv_sems, local_sems,
):
    row = lax.axis_index("row")
    y, core = row // 2, lax.rem(row, 2)
    col = lax.axis_index("col")
    z, x = col // 2, lax.rem(col, 2)
    f = lax.axis_index("feat")
    sib = {"row": y * 2 + 1 - core}
    yup = {"row": wrap(y + 1, 4) * 2 + core}
    ydown = {"row": wrap(y - 1, 4) * 2 + core}
    yfar = {"row": wrap(y + 2, 4) * 2 + core}
    other = {"feat": 1 - f}
    nbr = {"col": z * 2 + 1 - x}
    up = {"col": wrap(z + 1, 8) * 2 + x}
    down = {"col": wrap(z - 1, 8) * 2 + x}
    up_x = {"col": wrap(z + 1, 8) * 2 + 1 - x}
    down_x = {"col": wrap(z - 1, 8) * 2 + 1 - x}
    rows_of = [{"row": wrap(row + k, 8)} for k in range(1, 8)]
    cols_of = [{"col": wrap(col + k, 16)} for k in range(1, 16)]
    wait = greet(rows_of + cols_of + [other])
    net = Net(send_sems, recv_sems)
    A, B, ALL, THREE = pl.ds(0, 64), pl.ds(64, 64), pl.ds(0, 128), pl.ds(0, 3)

    fetches = []

    def fetch(src, dst):
        copy = pltpu.make_async_copy(src, dst, local_sems.at[len(fetches)])
        copy.start()
        fetches.append(copy)

    fetch(feat_ref, fall.at[row])
    fetch(w_ref, wfull.at[f])
    fetch(coord_ref, coord)
    fetch(bias_ref, bias)
    fetch(cot_ref, cot)
    for n in range(4):
        span = pl.ds(n * 48, 48)
        fetch(blocks_ref.at[span], blk.at[span])
    fetches[0].wait()
    fetches[1].wait()
    own = jnp.dot(fall[row].reshape(384, 256), wfull[f], preferred_element_type=F32).astype(BF)
    xw[row] = own.reshape(3, 128, 128)
    blk[192] = jnp.zeros((128, 128), BF)
    wait()

    def gather_row(buf):
        def move(slot, device, rows=ALL):
            ref = buf.at[slot, THREE, rows]
            return net.send(ref, ref, device)

        lower = wrap(y - 1, 4) * 2 + core
        upper = wrap(y + 1, 4) * 2 + core
        far = wrap(y + 2, 4) * 2 + core
        u0, d1 = move(row, yup, A), move(row, ydown, B)
        u1, d0 = move(row, yup, B), move(row, ydown, A)
        s = [move(row, sib)]
        yield
        u0.wait_recv()
        u2 = move(lower, yup, A)
        d1.wait_recv()
        d2 = move(upper, ydown, B)
        yield
        u1.wait_recv()
        s.append(move(lower, sib))
        d0.wait_recv()
        s.append(move(upper, sib))
        yield
        u2.wait_recv()
        d2.wait_recv()
        s.append(move(far, sib))
        yield
        for copy in s:
            copy.wait_recv()

    def order(n, key, targets):
        order_slots(coord, count_ref[0], key, targets, lists.at[n], work)
        fetch(lists.at[n], table.at[n])
        yield

    fetches[2].wait()
    interleave([gather_row(xw), order(0, 0, 48)])
    features_to_all = gather_row(fall)
    next(features_to_all)
    wcopy = net.send(wfull.at[f], wfull.at[f], other)
    for copy in fetches[3:]:
        copy.wait()
    fetches.clear()
    products(table.at[0], blk, xw.reshape(24, 128, 128), run_of, 120, 24, False)

    def summed(n, t):
        return jnp.where(table[n, 4, t] == 1, run_of[table[n, 3, t]], 0.0)

    starts = {}

    def place(k, side):
        shard = wrap(z + k, 8) * 2 + side
        for b in range(3):
            p[shard, b] = summed(0, shard * 3 + b).astype(BF)
        return shard

    shard, cross = place(4, x), place(4, 1 - x)
    for b in range(3):
        starts["u", b] = net.send(p.at[shard, b, A], rp.at[0, b, A], up)
        starts["d", b] = net.send(p.at[shard, b, B], rm.at[0, b, B], down)
        starts["u4", b] = net.send(p.at[cross, b, A], dp.at[0, b, A], up_x)
        starts["d4", b] = net.send(p.at[cross, b, B], dm.at[0, b, B], down_x)
    for name, k, landing, device in (("u3", 3, dp, up_x), ("d3", -3, dm, down_x)):
        shard = place(k, 1 - x)
        for b in range(3):
            starts[name, b] = net.send(p.at[shard, b], landing.at[1, b], device)
    for k in (2, -2, 1, -1, 0):
        shard = place(k, 1 - x)
        for b in range(3):
            starts[k, b] = net.send(p.at[shard, b], xr.at[k % 8, b], nbr)

    def own(k, b):
        return summed(0, (wrap(z + k, 8) * 2 + x) * 3 + b)

    def wide(ref):
        return ref.astype(F32)

    def reduce_col(b):
        u, d = starts["u", b], starts["d", b]
        u.wait_recv()
        starts["u4", b].wait_recv()
        value = own(3, b)
        sp[1, b, A] = (value[:64] + wide(rp[0, b, A]) + wide(dp[0, b, A])).astype(BF)
        sp[1, b, B] = value[64:].astype(BF)
        u = net.send(sp.at[1, b], rp.at[1, b], up)
        d.wait_recv()
        starts["d4", b].wait_recv()
        value = own(-3, b)
        sm[1, b, A] = value[:64].astype(BF)
        sm[1, b, B] = (value[64:] + wide(rm[0, b, B]) + wide(dm[0, b, B])).astype(BF)
        d = net.send(sm.at[1, b], rm.at[1, b], down)
        yield
        for t in (2, 3):
            k = 4 - t
            u.wait_recv()
            starts[k, b].wait_recv()
            value = own(k, b) + wide(xr[k, b]) + wide(rp[t - 1, b])
            if t == 2:
                starts["u3", b].wait_recv()
                value += wide(dp[1, b])
            sp[t, b] = value.astype(BF)
            u = net.send(sp.at[t, b], rp.at[t, b], up)
            d.wait_recv()
            starts[-k, b].wait_recv()
            value = own(-k, b) + wide(xr[8 - k, b]) + wide(rm[t - 1, b])
            if t == 2:
                starts["d3", b].wait_recv()
                value += wide(dm[1, b])
            sm[t, b] = value.astype(BF)
            d = net.send(sm.at[t, b], rm.at[t, b], down)
            yield
        starts[0, b].wait_recv()
        value = own(0, b) + wide(xr[0, b])
        u.wait_recv()
        d.wait_recv()
        return value + wide(rp[3, b]) + wide(rm[3, b])

    def activate(b, total):
        rows = pl.ds(b * 128, 128)
        pre = total + bias[...]
        s = 1.0 / (1.0 + jnp.exp(-pre))
        out_ref[rows] = (pre * s).astype(BF)
        gz = cot[rows].astype(F32) * s * (1.0 + pre * (1.0 - s))
        g[col, b] = gz.T.astype(BF)

    def gather_col(b):
        def move(slot, device, rows=ALL):
            ref = g.at[slot, b, rows]
            return net.send(ref, ref, device)

        rest = []
        last = {1: move(col, up), -1: move(col, down)}
        rest.append(move(col, nbr))
        for hop in range(1, 5):
            yield
            for sign, device, cross, rows in ((1, up, up_x, A), (-1, down, down_x, B)):
                slot = wrap(z - sign * hop, 8) * 2 + x
                last[sign].wait_recv()
                if hop < 4:
                    part = ALL if hop < 3 else rows
                    last[sign] = move(slot, device, part)
                    if hop < 3:
                        if hop == 2:
                            rest.append(move(slot, cross))
                        rest.append(move(slot, nbr))
                    else:
                        rest.append(move(slot, cross, rows))
        yield
        for copy in rest:
            copy.wait_recv()

    def stream(b):
        total = yield from reduce_col(b)
        activate(b, total)
        yield from gather_col(b)

    interleave([stream(0), stream(1), stream(2), order(1, 1, 24), features_to_all])
    fetches[0].wait()

    products(table.at[1], blk, g.reshape(48, 128, 128), run_of, 108, 27, True)

    to_core = {}
    for k in (2, 1, -1, 0):
        shard = wrap(y + k, 4) * 2 + 1 - core
        for b in range(3):
            p5[shard, b] = summed(1, shard * 3 + b).astype(BF)
        to_core[k] = net.send(p5.at[shard], cr.at[k % 4], sib)
    for k in (2, 1, -1, 0):
        shard = wrap(y + k, 4) * 2 + core
        for b in range(3):
            p5[shard, b] = summed(1, shard * 3 + b).astype(BF)

    def mine(k, b, rows):
        slot = wrap(y + k, 4) * 2 + core
        return p5[slot, b, rows].astype(F32) + cr[k % 4, b, rows].astype(F32)

    def input_gradient():
        far = {}
        for b in (1, 0, 2):
            for k, device in ((2, yfar), (1, yup), (-1, ydown)):
                if b == 1:
                    to_core[k].wait_recv()
                sp5[k % 4, b] = mine(k, b, ALL).astype(BF)
                far[k, b] = net.send(sp5.at[k % 4, b], rp5.at[k % 4, b], device)
        yield
        to_core[0].wait_recv()
        halves = []
        for b in (1, 0, 2):
            total = mine(0, b, ALL)
            for k in (1, -1, 2):
                far[k, b].wait_recv()
                total += rp5[k % 4, b].astype(F32)
            g5[b] = total.astype(BF)
            if b == 1:
                halves.append(net.send(g5.at[1], h.at[f], other))
        halves.append(net.send(g5.at[2 - 2 * f], h.at[1 - f], other))
        yield
        wcopy.wait_recv()
        for copy in halves:
            copy.wait_recv()
        for n in range(2):
            block = jnp.dot(wfull[f], g5[f + n], preferred_element_type=F32)
            block += jnp.dot(wfull[1 - f], h[n], preferred_element_type=F32)
            gin[pl.ds(n * 128, 128)] = block.T.astype(BF)
        gin_ref[...] = gin[pl.ds(pl.multiple_of(f * 64, 64), 192)]

    def weight_gradient():
        gwt = jnp.zeros((128, 256), F32)
        for j in range(0, 24, 2):
            a, b = (j // 3, j % 3), ((j + 1) // 3, (j + 1) % 3)
            lhs = jnp.concatenate([p5[a], p5[b]], axis=1)
            rhs = jnp.concatenate([fall[a], fall[b]], axis=0)
            gwt += jnp.dot(lhs, rhs, preferred_element_type=F32)
        for r in range(8):
            part5[r] = gwt[r * 16:(r + 1) * 16]
        copies = []
        for k in range(1, 8):
            copies.append(net.send(part5.at[wrap(row + k, 8)], w1.at[row], rows_of[k - 1]))
        w1[row] = part5[row]
        yield

        def add(t, total):
            return total + g[t // 3, lax.rem(t, 3)].astype(F32)

        nodes = lax.fori_loop(0, 48, add, jnp.zeros((128, 128), F32), unroll=4)
        bsend[...] = jnp.broadcast_to(jnp.sum(nodes.T, axis=0, keepdims=True), (8, 128))
        for copy in copies:
            copy.wait_recv()
        total = w1[0]
        for r in range(1, 8):
            total += w1[r]
        w2[col] = total.astype(BF)
        copies = [net.send(w2.at[col], w2.at[col], cols_of[k - 1]) for k in range(1, 16)]
        biases = [net.send(bsend, brecv.at[row], rows_of[k - 1]) for k in range(1, 8)]
        brecv[row] = bsend[...]
        yield
        for copy in copies:
            copy.wait_recv()
        total = w2[0].astype(F32)
        for c in range(1, 16):
            total += w2[c].astype(F32)
        w3[row] = total
        copies = [net.send(w3.at[row], w3.at[row], rows_of[k - 1]) for k in range(1, 8)]
        for copy in biases:
            copy.wait_recv()
        gb_ref[...] = jnp.sum(brecv[...], axis=0)[0:1]
        yield
        for copy in copies:
            copy.wait_recv()
        gw_ref[...] = w3[...].reshape(128, 256).T

    interleave([weight_gradient(), input_gradient()])
    net.drain()


def emit(*refs):
    for n in range(4):
        refs[4 + n][...] = refs[n][...]


def body(features, weight, bias, blocks, coords, counts, cotangent):
    shape = jax.ShapeDtypeStruct
    tile = (128, 128)

    def vmem(*dims, dtype=BF):
        return pltpu.VMEM(dims, dtype)

    copies = 200
    shapes = [
        shape((384, 128), BF), shape((192, 256), BF), shape((256, 128), F32), shape((1, 128), F32),
    ]
    results = pl.pallas_call(
        layer,
        out_shape=shapes,
        in_specs=[ANY, ANY, ANY, ANY, SMEM, ANY, ANY],
        out_specs=[VMEM] * 4,
        scratch_shapes=[
            vmem(8, 3, *tile), vmem(8, 3, 128, 256), vmem(2, 256, 128), vmem(193, *tile),
            vmem(120, *tile, dtype=F32), vmem(16, 3, *tile), vmem(16, 3, *tile),
            vmem(4, 3, *tile), vmem(4, 3, *tile), vmem(4, 3, *tile), vmem(4, 3, *tile),
            vmem(2, 3, *tile), vmem(2, 3, *tile), vmem(8, 3, *tile),
            vmem(8, 3, *tile), vmem(4, 3, *tile), vmem(4, 3, *tile), vmem(4, 3, *tile), vmem(3, *tile), vmem(2, *tile), vmem(256, 256),
            vmem(8, 16, 256, dtype=F32), vmem(8, 16, 256, dtype=F32), vmem(16, 16, 256),
            vmem(8, 16, 256, dtype=F32), vmem(8, 128, dtype=F32), vmem(8, 8, 128, dtype=F32),
            vmem(2, 192, dtype=jnp.int32), vmem(1, 128, dtype=F32), vmem(384, 128),
            vmem(8, 256, dtype=F32), vmem(2, 8, 256, dtype=jnp.int32),
            pltpu.SMEM((2, 8, 256), jnp.int32),
            pltpu.SemaphoreType.DMA((copies,)), pltpu.SemaphoreType.DMA((copies,)),
            pltpu.SemaphoreType.DMA((11,)),
        ],
        compiler_params=pltpu.CompilerParams(
            collective_id=1, has_side_effects=True, vmem_limit_bytes=LIMIT
        ),
        name="layer",
    )(
        features.reshape(3, 128, 256), weight, bias.reshape(1, 128), coords[0, 0].T, counts[0],
        cotangent, blocks[0, 0],
    )
    outputs, grad_in, grad_w, grad_b = pl.pallas_call(
        emit,
        out_shape=shapes,
        in_specs=[VMEM] * 4,
        out_specs=[VMEM] * 4,
        name="emit",
    )(*results)
    return outputs, grad_in, grad_w, grad_b.reshape(128)


def solution(mesh):
    in_specs = (
        P(("col", "row"), None),
        P(None, "feat"),
        P("feat"),
        P("row", "col", None, None, None),
        P("row", "col", None, None),
        P("row", "col"),
        P(("row", "col"), "feat"),
    )
    out_specs = (
        P(("row", "col"), "feat"),
        P(("col", "row", "feat"), None),
        P(None, "feat"),
        P("feat"),
    )
    return jax.shard_map(body, mesh=mesh, in_specs=in_specs, out_specs=out_specs, check_vma=False)
```

time: 1320 us -> 85.5 us (0.06)
  waiting for transfers between devices: 907 us -> 0 us
  blocking collectives: 261 us -> 0 us
  Pallas kernels: 0 us -> 84.1 us
  other arithmetic: 54.6 us -> 0 us
  local copies, waits for them, and re-layouts: 47.9 us -> 0 us
  matrix products: 30.7 us -> 0 us
  between operations: 14.8 us -> 1.29 us
    psum x1 -> x0, waiting for transfers between devices: 661 us -> none  [body(): grad_w, grad_b = lax.psum((weight_part, bias_part), ('row', 'col'))]
    psum x1 -> x0, blocking collectives: 261 us -> none  [body(): grad_w, grad_b = lax.psum((weight_part, bias_part), ('row', 'col'))]
    reduce_scatter x3 -> x0, waiting for transfers between devices: 149 us -> none  [the longest x1 76.8 us: body(): lax.psum_scatter(partial_value, 'col', scatter_dimension=0, tiled=True)]
    all_gather x2 -> x0, waiting for transfers between devices: 96.2 us -> none  [the longest x1 64.6 us: body(): row_grads = lax.all_gather(grad_z, 'col', axis=0, tiled=True)]
    pallas_call x0 -> x2, Pallas kernels: none -> 84.1 us  [the longest x1 82.4 us: body(): pl.pallas_call(layer, out_shape=shapes, in_specs=[ANY, ANY, ANY, ANY, SME...]
    scatter-add x2 -> x0, other arithmetic: 50.6 us -> none  [spread(): jax.ops.segment_sum(products, targets, num_segments=segment_count + 1)]
    dot_general x5 -> x0, matrix products: 30.7 us -> none  [the longest x2 25.1 us: spread(): jnp.einsum(einsum_form, block_set, pieces, preferred_element_type=jnp.flo...]
    dot_general x2 -> x0, local copies, waits for them, and re-layouts: 25.2 us -> none  [spread(): jnp.einsum(einsum_form, block_set, pieces, preferred_element_type=jnp.flo...]
  transfers between devices with their start and end apart: 6 -> 0, of which waited for: 6 -> 0; matrix products, arithmetic and copies ran while one was open for 0% -> 0% of each run, Pallas kernels for 0% -> 0%
where the time goes in v2:
time: 85.5 us; the launch traced here: 85.4 us
  Pallas kernels  84.1 us (98%)
  between operations  1.29 us (2%)
    pallas_call x1, Pallas kernels, body(): pl.pallas_call(layer, out_shape=shapes, in_specs=[ANY, ANY, ANY, ANY, SME...  82.4 us
    pallas_call x1, Pallas kernels, body(): pl.pallas_call(emit, out_shape=shapes, in_specs=[VMEM] * 4, out_specs=[VM...  1.73 us

profile of v2, /device:TPU:1, one launch (start us, length us, event | category | flops | bytes accessed | tf_op | source)
XLA Modules:
  0.0 85.4 jit_solution(13889987818931939731)
XLA Ops:
  1.3 82.4 %layer.1 = (bf16[384,128]{1,0:T(8,128)(2,1)}, bf16[192,256]{1,0:T(8,128)(2,1)}, f32[256,128]{1,0:T(8,128)}, f32[1,128]{1,0:T(1,128)}) custom-call(bf16[3,128,256]{2,1,0:T(8,128)(2,1)} %bitcast.10, bf16[256,128]{1,0:T(8,128)(2,1)} %w_ref.1, f32[1,128]{1,0:T(1,128)} %bitcast.12, s32[2,192]{1,0:T(2,128)} %bitcast.11, s32[1]{0:T(128)} %bitcast.8.count_ref, ...), custom_call_target="tpu_custom_call" | custom-call | tf_op jit(solution)/shard_map/layer/pallas_call | solution.py:445
  83.7 1.7 %emit.1 = (bf16[384,128]{1,0:T(8,128)(2,1)}, bf16[192,256]{1,0:T(8,128)(2,1)}, f32[256,128]{1,0:T(8,128)}, f32[1,128]{1,0:T(1,128)}) custom-call(bf16[384,128]{1,0:T(8,128)(2,1)} %get-tuple-element.12.refs_0_, bf16[192,256]{1,0:T(8,128)(2,1)} %get-tuple-element.13.refs_1_, f32[256,128]{1,0:T(8,128)} %get-tuple-element.14.refs_2_, ...), custom_call_target="tpu_custom_call" | custom-call | tf_op jit(solution)/shard_map/emit/pallas_call | solution.py:472

commit v3 on v2

--- a/solution.py
+++ b/solution.py
@@ -18,7 +18,7 @@
 
 class Net:
     def __init__(self, send_sems, recv_sems):
-        self.send_sems, self.recv_sems, self.copies = send_sems, recv_sems, []
+        self.send_sems, self.recv_sems, self.copies, self.drained = send_sems, recv_sems, [], 0
 
     def send(self, src, dst, device):
         index = len(self.copies)
@@ -34,9 +34,11 @@
         self.copies.append(copy)
         return copy
 
-    def drain(self):
-        for copy in self.copies:
+    def drain(self, end=None):
+        end = len(self.copies) if end is None else end
+        for copy in self.copies[self.drained:end]:
             copy.wait_send()
+        self.drained = end
 
 
 def greet(devices):
@@ -173,32 +175,35 @@
     wait()
 
     def gather_row(buf):
-        def move(slot, device, rows=ALL):
-            ref = buf.at[slot, THREE, rows]
+        def move(slot, device, b, rows=ALL):
+            ref = buf.at[slot, b, rows]
             return net.send(ref, ref, device)
 
         lower = wrap(y - 1, 4) * 2 + core
         upper = wrap(y + 1, 4) * 2 + core
         far = wrap(y + 2, 4) * 2 + core
-        u0, d1 = move(row, yup, A), move(row, ydown, B)
-        u1, d0 = move(row, yup, B), move(row, ydown, A)
-        s = [move(row, sib)]
-        yield
-        u0.wait_recv()
-        u2 = move(lower, yup, A)
-        d1.wait_recv()
-        d2 = move(upper, ydown, B)
-        yield
-        u1.wait_recv()
-        s.append(move(lower, sib))
-        d0.wait_recv()
-        s.append(move(upper, sib))
-        yield
-        u2.wait_recv()
-        d2.wait_recv()
-        s.append(move(far, sib))
-        yield
-        for copy in s:
+        ups, downs, rest, far_u, far_d = {}, {}, [], {}, {}
+        for bu, bd in ((0, 2), (1, 1), (2, 0)):
+            ups[bu] = move(row, yup, bu)
+            downs[bd] = move(row, ydown, bd)
+        for b in range(3):
+            rest.append(move(row, sib, b))
+        yield
+        for bu, bd in ((0, 2), (1, 1), (2, 0)):
+            ups[bu].wait_recv()
+            if bu < 2:
+                far_u[bu] = move(lower, yup, bu, ALL if bu == 0 else A)
+            rest.append(move(lower, sib, bu))
+            downs[bd].wait_recv()
+            if bd > 0:
+                far_d[bd] = move(upper, ydown, bd, ALL if bd == 2 else B)
+            rest.append(move(upper, sib, bd))
+        yield
+        for copies, b, rows in ((far_u, 0, ALL), (far_d, 2, ALL), (far_u, 1, A), (far_d, 1, B)):
+            copies[b].wait_recv()
+            rest.append(move(far, sib, b, rows))
+        yield
+        for copy in rest:
             copy.wait_recv()
 
     def order(n, key, targets):
@@ -385,7 +390,7 @@
             rhs = jnp.concatenate([fall[a], fall[b]], axis=0)
             gwt += jnp.dot(lhs, rhs, preferred_element_type=F32)
         for r in range(8):
-            part5[r] = gwt[r * 16:(r + 1) * 16]
+            part5[r] = gwt[r * 16:(r + 1) * 16].astype(BF)
         copies = []
         for k in range(1, 8):
             copies.append(net.send(part5.at[wrap(row + k, 8)], w1.at[row], rows_of[k - 1]))
@@ -399,13 +404,15 @@
         bsend[...] = jnp.broadcast_to(jnp.sum(nodes.T, axis=0, keepdims=True), (8, 128))
         for copy in copies:
             copy.wait_recv()
-        total = w1[0]
+        total = w1[0].astype(F32)
         for r in range(1, 8):
-            total += w1[r]
+            total += w1[r].astype(F32)
         w2[col] = total.astype(BF)
+        before = len(net.copies)
         copies = [net.send(w2.at[col], w2.at[col], cols_of[k - 1]) for k in range(1, 16)]
         biases = [net.send(bsend, brecv.at[row], rows_of[k - 1]) for k in range(1, 8)]
         brecv[row] = bsend[...]
+        net.drain(before)
         yield
         for copy in copies:
             copy.wait_recv()
@@ -417,6 +424,7 @@
         for copy in biases:
             copy.wait_recv()
         gb_ref[...] = jnp.sum(brecv[...], axis=0)[0:1]
+        net.drain(len(net.copies) - 7)
         yield
         for copy in copies:
             copy.wait_recv()
@@ -453,7 +461,7 @@
             vmem(4, 3, *tile), vmem(4, 3, *tile), vmem(4, 3, *tile), vmem(4, 3, *tile),
             vmem(2, 3, *tile), vmem(2, 3, *tile), vmem(8, 3, *tile),
             vmem(8, 3, *tile), vmem(4, 3, *tile), vmem(4, 3, *tile), vmem(4, 3, *tile), vmem(3, *tile), vmem(2, *tile), vmem(256, 256),
-            vmem(8, 16, 256, dtype=F32), vmem(8, 16, 256, dtype=F32), vmem(16, 16, 256),
+            vmem(8, 16, 256), vmem(8, 16, 256), vmem(16, 16, 256),
             vmem(8, 16, 256, dtype=F32), vmem(8, 128, dtype=F32), vmem(8, 8, 128, dtype=F32),
             vmem(2, 192, dtype=jnp.int32), vmem(1, 128, dtype=F32), vmem(384, 128),
             vmem(8, 256, dtype=F32), vmem(2, 8, 256, dtype=jnp.int32),

time: 85.5 us -> 84 us (0.982)
  Pallas kernels: 84.1 us -> 82.6 us
    pallas_call x1, Pallas kernels: 82.4 us -> 80.9 us  [body(): pl.pallas_call(layer, out_shape=shapes, in_specs=[ANY, ANY, ANY, ANY, SME...]
where the time goes in v3:
time: 84 us; the launch traced here: 83.9 us
  Pallas kernels  82.6 us (98%)
  between operations  1.29 us (2%)
    pallas_call x1, Pallas kernels, body(): pl.pallas_call(layer, out_shape=shapes, in_specs=[ANY, ANY, ANY, ANY, SME...  80.9 us
    pallas_call x1, Pallas kernels, body(): pl.pallas_call(emit, out_shape=shapes, in_specs=[VMEM] * 4, out_specs=[VM...  1.73 us

profile of v3, /device:TPU:1, one launch (start us, length us, event | category | flops | bytes accessed | tf_op | source)
XLA Modules:
  0.0 83.9 jit_solution(16111492833775566902)
XLA Ops:
  1.3 80.9 %layer.1 = (bf16[384,128]{1,0:T(8,128)(2,1)}, bf16[192,256]{1,0:T(8,128)(2,1)}, f32[256,128]{1,0:T(8,128)}, f32[1,128]{1,0:T(1,128)}) custom-call(bf16[3,128,256]{2,1,0:T(8,128)(2,1)} %bitcast.10, bf16[256,128]{1,0:T(8,128)(2,1)} %w_ref.1, f32[1,128]{1,0:T(1,128)} %bitcast.12, s32[2,192]{1,0:T(2,128)} %bitcast.11, s32[1]{0:T(128)} %bitcast.8.count_ref, ...), custom_call_target="tpu_custom_call" | custom-call | tf_op jit(solution)/shard_map/layer/pallas_call | solution.py:453
  82.2 1.7 %emit.1 = (bf16[384,128]{1,0:T(8,128)(2,1)}, bf16[192,256]{1,0:T(8,128)(2,1)}, f32[256,128]{1,0:T(8,128)}, f32[1,128]{1,0:T(1,128)}) custom-call(bf16[384,128]{1,0:T(8,128)(2,1)} %get-tuple-element.12.refs_0_, bf16[192,256]{1,0:T(8,128)(2,1)} %get-tuple-element.13.refs_1_, f32[256,128]{1,0:T(8,128)} %get-tuple-element.14.refs_2_, ...), custom_call_target="tpu_custom_call" | custom-call | tf_op jit(solution)/shard_map/emit/pallas_call | solution.py:480

commit v4 on v3

--- a/solution.py
+++ b/solution.py
@@ -129,6 +129,7 @@
     out_ref, gin_ref, gw_ref, gb_ref,
     xw, fall, wfull, blk, run_of, p, g, rp, rm, sp, sm, dp, dm, xr,
     p5, cr, rp5, sp5, g5, h, gin, part5, w1, w2, w3, bsend, brecv,
+    wide_of, agg, carry,
     coord, bias, cot, work, lists, table, send_sems, recv_sems, local_sems,
 ):
     row = lax.axis_index("row")
@@ -206,6 +207,21 @@
         for copy in rest:
             copy.wait_recv()
 
+    def gather_row_direct(buf):
+        def move(slot, device):
+            ref = buf.at[slot]
+            return net.send(ref, ref, device)
+
+        far, upper, lower = move(row, yfar), move(row, yup), move(row, ydown)
+        rest = [move(row, sib)]
+        yield
+        for copy, k in ((upper, -1), (lower, 1), (far, 2)):
+            copy.wait_recv()
+            rest.append(move(wrap(y + k, 4) * 2 + core, sib))
+        yield
+        for copy in rest:
+            copy.wait_recv()
+
     def order(n, key, targets):
         order_slots(coord, count_ref[0], key, targets, lists.at[n], work)
         fetch(lists.at[n], table.at[n])
@@ -213,7 +229,7 @@
 
     fetches[2].wait()
     interleave([gather_row(xw), order(0, 0, 48)])
-    features_to_all = gather_row(fall)
+    features_to_all = gather_row_direct(fall)
     next(features_to_all)
     wcopy = net.send(wfull.at[f], wfull.at[f], other)
     for copy in fetches[3:]:
@@ -332,9 +348,91 @@
         activate(b, total)
         yield from gather_col(b)
 
-    interleave([stream(0), stream(1), stream(2), order(1, 1, 24), features_to_all])
+    def aggregate():
+        fa = fall.reshape(24, 128, 256)
+        for _ in features_to_all:
+            pass
+        carry[...] = jnp.zeros((128, 256), F32)
+
+        def group(i, run):
+            for u in range(10):
+                q = i * 10 + u
+                s0, s1 = table[0, 0, 2 * q], table[0, 0, 2 * q + 1]
+                t0, t1 = table[0, 1, 2 * q], table[0, 1, 2 * q + 1]
+                lhs = jnp.concatenate([blk[s0], blk[s1]], axis=1)
+                rhs = jnp.concatenate([fa[t0], fa[t1]], axis=0)
+                prod = jnp.dot(lhs, rhs, preferred_element_type=F32)
+                run = jnp.where(table[0, 2, 2 * q] == 1, 0.0, run) + prod
+                wide_of[q] = run
+            return run
+
+        for piece in range(6):
+            carry[...] = lax.fori_loop(piece * 2, piece * 2 + 2, group, carry[...])
+            yield
+
+        def pick(t, c):
+            value = wide_of[table[0, 3, t]]
+            agg[t] = jnp.where(table[0, 4, t] == 1, value, 0.0).astype(BF)
+            return c
+
+        for piece in range(2):
+            lax.fori_loop(piece * 24, piece * 24 + 24, pick, 0, unroll=4)
+            yield
+
+    next(features_to_all)
+    interleave([stream(0), stream(1), stream(2), order(1, 1, 24), aggregate()])
     fetches[0].wait()
 
+    def weight_gradient():
+        gwt = jnp.zeros((128, 256), F32)
+        gt = g.reshape(48, 128, 128)
+        for j in range(0, 48, 2):
+            lhs = jnp.concatenate([gt[j], gt[j + 1]], axis=1)
+            rhs = jnp.concatenate([agg[j], agg[j + 1]], axis=0)
+            gwt += jnp.dot(lhs, rhs, preferred_element_type=F32)
+        for r in range(8):
+            part5[r] = gwt[r * 16:(r + 1) * 16].astype(BF)
+        copies = []
+        for k in range(1, 8):
+            copies.append(net.send(part5.at[wrap(row + k, 8)], w1.at[row], rows_of[k - 1]))
+        w1[row] = part5[row]
+        yield
+
+        def add(t, total):
+            return total + g[t // 3, lax.rem(t, 3)].astype(F32)
+
+        nodes = lax.fori_loop(0, 48, add, jnp.zeros((128, 128), F32), unroll=4)
+        bsend[...] = jnp.broadcast_to(jnp.sum(nodes.T, axis=0, keepdims=True), (8, 128))
+        for copy in copies:
+            copy.wait_recv()
+        total = w1[0].astype(F32)
+        for r in range(1, 8):
+            total += w1[r].astype(F32)
+        w2[col] = total.astype(BF)
+        before = len(net.copies)
+        copies = [net.send(w2.at[col], w2.at[col], cols_of[k - 1]) for k in range(1, 16)]
+        biases = [net.send(bsend, brecv.at[row], rows_of[k - 1]) for k in range(1, 8)]
+        brecv[row] = bsend[...]
+        net.drain(before)
+        yield
+        for copy in copies:
+            copy.wait_recv()
+        total = w2[0].astype(F32)
+        for c in range(1, 16):
+            total += w2[c].astype(F32)
+        w3[row] = total
+        copies = [net.send(w3.at[row], w3.at[row], rows_of[k - 1]) for k in range(1, 8)]
+        for copy in biases:
+            copy.wait_recv()
+        gb_ref[...] = jnp.sum(brecv[...], axis=0)[0:1]
+        net.drain(len(net.copies) - 7)
+        yield
+        for copy in copies:
+            copy.wait_recv()
+        gw_ref[...] = w3[...].reshape(128, 256).T
+
+    weight_stream = weight_gradient()
+    next(weight_stream)
     products(table.at[1], blk, g.reshape(48, 128, 128), run_of, 108, 27, True)
 
     to_core = {}
@@ -382,55 +480,7 @@
             gin[pl.ds(n * 128, 128)] = block.T.astype(BF)
         gin_ref[...] = gin[pl.ds(pl.multiple_of(f * 64, 64), 192)]
 
-    def weight_gradient():
-        gwt = jnp.zeros((128, 256), F32)
-        for j in range(0, 24, 2):
-            a, b = (j // 3, j % 3), ((j + 1) // 3, (j + 1) % 3)
-            lhs = jnp.concatenate([p5[a], p5[b]], axis=1)
-            rhs = jnp.concatenate([fall[a], fall[b]], axis=0)
-            gwt += jnp.dot(lhs, rhs, preferred_element_type=F32)
-        for r in range(8):
-            part5[r] = gwt[r * 16:(r + 1) * 16].astype(BF)
-        copies = []
-        for k in range(1, 8):
-            copies.append(net.send(part5.at[wrap(row + k, 8)], w1.at[row], rows_of[k - 1]))
-        w1[row] = part5[row]
-        yield
-
-        def add(t, total):
-            return total + g[t // 3, lax.rem(t, 3)].astype(F32)
-
-        nodes = lax.fori_loop(0, 48, add, jnp.zeros((128, 128), F32), unroll=4)
-        bsend[...] = jnp.broadcast_to(jnp.sum(nodes.T, axis=0, keepdims=True), (8, 128))
-        for copy in copies:
-            copy.wait_recv()
-        total = w1[0].astype(F32)
-        for r in range(1, 8):
-            total += w1[r].astype(F32)
-        w2[col] = total.astype(BF)
-        before = len(net.copies)
-        copies = [net.send(w2.at[col], w2.at[col], cols_of[k - 1]) for k in range(1, 16)]
-        biases = [net.send(bsend, brecv.at[row], rows_of[k - 1]) for k in range(1, 8)]
-        brecv[row] = bsend[...]
-        net.drain(before)
-        yield
-        for copy in copies:
-            copy.wait_recv()
-        total = w2[0].astype(F32)
-        for c in range(1, 16):
-            total += w2[c].astype(F32)
-        w3[row] = total
-        copies = [net.send(w3.at[row], w3.at[row], rows_of[k - 1]) for k in range(1, 8)]
-        for copy in biases:
-            copy.wait_recv()
-        gb_ref[...] = jnp.sum(brecv[...], axis=0)[0:1]
-        net.drain(len(net.copies) - 7)
-        yield
-        for copy in copies:
-            copy.wait_recv()
-        gw_ref[...] = w3[...].reshape(128, 256).T
-
-    interleave([weight_gradient(), input_gradient()])
+    interleave([input_gradient(), weight_stream])
     net.drain()
 
 
@@ -463,6 +513,7 @@
             vmem(8, 3, *tile), vmem(4, 3, *tile), vmem(4, 3, *tile), vmem(4, 3, *tile), vmem(3, *tile), vmem(2, *tile), vmem(256, 256),
             vmem(8, 16, 256), vmem(8, 16, 256), vmem(16, 16, 256),
             vmem(8, 16, 256, dtype=F32), vmem(8, 128, dtype=F32), vmem(8, 8, 128, dtype=F32),
+            vmem(120, 128, 256, dtype=F32), vmem(48, 128, 256), vmem(128, 256, dtype=F32),
             vmem(2, 192, dtype=jnp.int32), vmem(1, 128, dtype=F32), vmem(384, 128),
             vmem(8, 256, dtype=F32), vmem(2, 8, 256, dtype=jnp.int32),
             pltpu.SMEM((2, 8, 256), jnp.int32),

time: 84 us -> 83.2 us (level)
  no operation moved by 1% of the time
where the time goes in v4:
time: 83.2 us; the launch traced here: 83.1 us
  Pallas kernels  81.8 us (98%)
  between operations  1.29 us (2%)
    pallas_call x1, Pallas kernels, body(): pl.pallas_call(layer, out_shape=shapes, in_specs=[ANY, ANY, ANY, ANY, SME...  80.1 us
    pallas_call x1, Pallas kernels, body(): pl.pallas_call(emit, out_shape=shapes, in_specs=[VMEM] * 4, out_specs=[VM...  1.73 us

profile of v4, /device:TPU:1, one launch (start us, length us, event | category | flops | bytes accessed | tf_op | source)
XLA Modules:
  0.0 83.1 jit_solution(5653920888098943473)
XLA Ops:
  1.3 80.1 %layer.1 = (bf16[384,128]{1,0:T(8,128)(2,1)}, bf16[192,256]{1,0:T(8,128)(2,1)}, f32[256,128]{1,0:T(8,128)}, f32[1,128]{1,0:T(1,128)}) custom-call(bf16[3,128,256]{2,1,0:T(8,128)(2,1)} %bitcast.10, bf16[256,128]{1,0:T(8,128)(2,1)} %w_ref.1, f32[1,128]{1,0:T(1,128)} %bitcast.12, s32[2,192]{1,0:T(2,128)} %bitcast.11, s32[1]{0:T(128)} %bitcast.8.count_ref, ...), custom_call_target="tpu_custom_call" | custom-call | tf_op jit(solution)/shard_map/layer/pallas_call | solution.py:503
  81.4 1.7 %emit.1 = (bf16[384,128]{1,0:T(8,128)(2,1)}, bf16[192,256]{1,0:T(8,128)(2,1)}, f32[256,128]{1,0:T(8,128)}, f32[1,128]{1,0:T(1,128)}) custom-call(bf16[384,128]{1,0:T(8,128)(2,1)} %get-tuple-element.12.refs_0_, bf16[192,256]{1,0:T(8,128)(2,1)} %get-tuple-element.13.refs_1_, f32[256,128]{1,0:T(8,128)} %get-tuple-element.14.refs_2_, ...), custom_call_target="tpu_custom_call" | custom-call | tf_op jit(solution)/shard_map/emit/pallas_call | solution.py:531
